TPU v7x, 128 devices: a whole 4x4x4 slice. The times are simulated.
128 devices in a mesh: span: 16 (over y, z), wall: 8 (over x, core).
Axes of the slice: x: 4, y: 4, z: 4, core: 2. Of those that a mesh axis runs over, the one named last changes fastest.
Arguments:
- stress: float32 [2, 32, 1024, 2048], P(None, None, 'wall', 'span'), may hold values from -8 to 8
Outputs:
- pressure: float32 [2, 32, 1024, 2048], P(None, None, 'wall', 'span')
All inputs are finite; a program needn't handle non-finite values.
Results may differ from a plain program's by a relative error of at most 0.00035.
Values sent between devices are 32-bit elements; how exact they have to be, the bound alone decides.
A program may use at most 128 MiB of HBM per device.

v0:
```python
import math
import jax
import jax.numpy as jnp
from jax import lax
from jax.sharding import PartitionSpec as P

stretch_rate = 2.0
span_rate = 2.0 / 3.0
stream_rate = 0.25


def shifted(array, axis, by):
    peers = lax.axis_size(axis)
    pairs = [(i, i + by) for i in range(peers) if 0 <= i + by < peers]
    return lax.ppermute(array, axis, pairs)


def wall_coefficients(count):
    node_index = jnp.arange(count + 1, dtype=jnp.int32)
    xi_left = (2 * node_index - count - 1).astype(jnp.float32) / (count + 1)
    xi_right = (2 * node_index - count + 1).astype(jnp.float32) / (count + 1)
    spacing = jnp.sinh(2.0 * stretch_rate / (count + 1)) / (
        jnp.tanh(stretch_rate)
        * jnp.cosh(stretch_rate * xi_left)
        * jnp.cosh(stretch_rate * xi_right)
    )
    gap_before = spacing[:-1]
    gap_after = spacing[1:]
    lower_band = gap_after / (gap_before + gap_after)
    upper_band = gap_before / (gap_before + gap_after)
    weight = 0.5 * gap_before * gap_after
    return (lower_band, upper_band, weight)


def wave_squares(length, block_width, mode_ids):
    mode_index = jnp.arange(block_width, dtype=jnp.int32)
    signed = jnp.where(mode_index >= length // 2, mode_index - length, mode_index)
    span_wave = signed.astype(jnp.float32) * span_rate
    stream_wave = mode_ids.astype(jnp.float32) * stream_rate
    wave_sq = stream_wave[:, None] ** 2 + span_wave[None, :] ** 2
    return (wave_sq, span_wave**2)


def thomas(lower_band, upper_band, weight, wave_sq, rows):

    def forward(state, row_data):
        ratio_prev, value_prev = state
        low_entry, upp_entry, wei_entry, row_now = row_data
        pivot_value = 1.0 + wave_sq * wei_entry + low_entry * ratio_prev
        ratio_new = -upp_entry / pivot_value
        value_new = (row_now + low_entry * value_prev) / pivot_value
        return ((ratio_new, value_new), (ratio_new, value_new))

    start_state = (jnp.zeros(rows.shape[2:], jnp.float32), jnp.zeros(rows.shape[1:], jnp.float32))
    final_state, sweeps = lax.scan(
        forward, start_state, (lower_band, upper_band, weight, rows), unroll=4
    )

    def backward(after_value, row_data):
        ratio_now, value_now = row_data
        value_here = value_now - ratio_now[None] * after_value
        return (value_here, value_here)

    final_value, solution = lax.scan(
        backward, jnp.zeros(rows.shape[1:], jnp.float32), sweeps, reverse=True, unroll=4
    )
    return solution


def factor_pair(length):
    factor = 1
    for divisor in range(1, math.isqrt(length) + 1):
        if length % divisor == 0:
            factor = divisor
    return (factor, length // factor)


def phase_table(row_count, col_count, length, sign):
    row_ids = jnp.arange(row_count, dtype=jnp.int32)[:, None]
    col_ids = jnp.arange(col_count, dtype=jnp.int32)[None, :]
    angle_table = (row_ids * col_ids % length).astype(jnp.float32) * (2.0 * math.pi / length)
    return (jnp.cos(angle_table), sign * jnp.sin(angle_table))


def factored_dft(real_in, imag_in, sign):
    length = real_in.shape[-1]
    inner_len, outer_len = factor_pair(length)
    leading = real_in.shape[:-1]
    real_grid = real_in.reshape(leading + (outer_len, inner_len))
    imag_grid = imag_in.reshape(leading + (outer_len, inner_len))
    cos_outer, sin_outer = phase_table(outer_len, outer_len, outer_len, sign)
    high = lax.Precision.HIGHEST
    first_real = jnp.einsum("...za,zm->...ma", real_grid, cos_outer, precision=high) - jnp.einsum(
        "...za,zm->...ma", imag_grid, sin_outer, precision=high
    )
    first_imag = jnp.einsum("...za,zm->...ma", real_grid, sin_outer, precision=high) + jnp.einsum(
        "...za,zm->...ma", imag_grid, cos_outer, precision=high
    )
    cos_twid, sin_twid = phase_table(outer_len, inner_len, length, sign)
    twid_real = first_real * cos_twid - first_imag * sin_twid
    twid_imag = first_real * sin_twid + first_imag * cos_twid
    cos_inner, sin_inner = phase_table(inner_len, inner_len, inner_len, sign)
    last_real = jnp.einsum("...ma,an->...nm", twid_real, cos_inner, precision=high) - jnp.einsum(
        "...ma,an->...nm", twid_imag, sin_inner, precision=high
    )
    last_imag = jnp.einsum("...ma,an->...nm", twid_real, sin_inner, precision=high) + jnp.einsum(
        "...ma,an->...nm", twid_imag, cos_inner, precision=high
    )
    return (last_real.reshape(leading + (length,)), last_imag.reshape(leading + (length,)))


def body(stress):
    mode_count = stress.shape[1]
    rows_dev = stress.shape[2]
    span_count = lax.axis_size("span")
    wall_count = lax.axis_size("wall")
    mode_dev = mode_count // span_count
    length = stress.shape[3] * span_count
    wall_cells = rows_dev * wall_count
    wall_at = lax.axis_index("wall")
    span_at = lax.axis_index("span")
    lower_all, upper_all, weight_all = wall_coefficients(wall_cells)
    row_start = wall_at * rows_dev
    lower_band = lax.dynamic_slice_in_dim(lower_all, row_start, rows_dev)
    upper_band = lax.dynamic_slice_in_dim(upper_all, row_start, rows_dev)
    weight = lax.dynamic_slice_in_dim(weight_all, row_start, rows_dev)
    mode_ids = span_at * mode_dev + jnp.arange(mode_dev, dtype=jnp.int32)
    wave_sq, span_sq = wave_squares(length, length, mode_ids)
    received = lax.all_to_all(stress, "span", split_axis=1, concat_axis=3, tiled=True)
    real_part, imag_part = factored_dft(received[0], received[1], -1.0)
    stacked = jnp.stack([real_part, imag_part], axis=0)
    spectral = jnp.transpose(stacked, (2, 0, 1, 3))
    source = spectral * weight[:, None, None, None] * span_sq[None, None, None, :]
    inner = rows_dev - 1
    row_index = jnp.arange(inner, dtype=jnp.int32)
    alpha_col = jnp.where(row_index == 0, lower_band[0], 0.0)
    beta_col = jnp.where(row_index == inner - 1, upper_band[inner - 1], 0.0)
    upper_inner = jnp.where(row_index == inner - 1, 0.0, upper_band[:inner])
    ones_block = jnp.ones((inner, 1, mode_dev, length), jnp.float32)
    extended = jnp.concatenate(
        [
            source[:inner],
            ones_block * alpha_col[:, None, None, None],
            ones_block * beta_col[:, None, None, None],
        ],
        axis=1,
    )
    local_part = thomas(lower_band[:inner], upper_inner, weight[:inner], wave_sq, extended)
    next_rows = shifted(local_part[0], "wall", -1)
    last_rows = local_part[inner - 1]
    sep_lower = lower_band[inner]
    sep_upper = upper_band[inner]
    sep_diag = 1.0 + wave_sq * weight[inner]
    coef_a = -sep_lower * last_rows[2]
    coef_b = sep_diag - sep_lower * last_rows[3] - sep_upper * next_rows[2]
    coef_c = -sep_upper * next_rows[3]
    coef_r = source[inner] + sep_lower * last_rows[0:2] + sep_upper * next_rows[0:2]
    levels = wall_count.bit_length() - 1
    for level in range(levels):
        stride = 1 << level
        packed = jnp.concatenate([coef_a[None], coef_b[None], coef_c[None], coef_r], axis=0)
        below_rows = shifted(packed, "wall", stride)
        above_rows = shifted(packed, "wall", -stride)
        below_pivot = below_rows[1] + (wall_at < stride).astype(jnp.float32)
        above_pivot = above_rows[1] + (wall_at + stride >= wall_count).astype(jnp.float32)
        left_factor = coef_a / below_pivot
        right_factor = coef_c / above_pivot
        new_a = -left_factor * below_rows[0]
        new_c = -right_factor * above_rows[2]
        new_b = coef_b - left_factor * below_rows[2] - right_factor * above_rows[0]
        new_r = coef_r - left_factor[None] * below_rows[3:5] - right_factor[None] * above_rows[3:5]
        coef_a, coef_b, coef_c, coef_r = (new_a, new_b, new_c, new_r)
    value_here = coef_r / coef_b[None]
    value_prev = shifted(value_here, "wall", 1)
    inner_rows = (
        local_part[:, 0:2]
        + local_part[:, 2:3] * value_prev[None]
        + local_part[:, 3:4] * value_here[None]
    )
    pressure_rows = jnp.concatenate([inner_rows, value_here[None]], axis=0)
    back_real, back_imag = factored_dft(pressure_rows[:, 0], pressure_rows[:, 1], 1.0)
    stacked = jnp.stack([back_real / length, back_imag / length], axis=0)
    physical = jnp.transpose(stacked, (0, 2, 1, 3))
    return lax.all_to_all(physical, "span", split_axis=3, concat_axis=1, tiled=True)


def solution(mesh):
    placed = (P(None, None, "wall", "span"),)
    return jax.shard_map(
        body, mesh=mesh, in_specs=placed, out_specs=P(None, None, "wall", "span"), check_vma=False
    )
```

profile of v0, /device:TPU:1, one launch (start us, length us, event | category | flops | bytes accessed | tf_op | source)
XLA Modules:
  0.0 899.3 jit_solution(15733420314305276271)
XLA Ops:
  4.7 8.6 all-to-all-start
  20.8 54.0 %all-to-all-done = f32[2,32,128,128]{3,2,0,1:T(8,128)} async-done(((f32[2,32,128,128]{3,2,0,1:T(8,128)}), f32[2,32,128,128]{3,2,0,1:T(8,128)}, u32[]{:S(2)}, u32[]{:S(2)}) %all-to-all-start) | async-done | bytes 4194336 | tf_op jit(solution)/shard_map/all_to_all | solution.py:129
  119.6 13.7 %slice_reduce_fusion.2 = (f32[4,2,2048]{2,1,0:T(2,128)S(1)}, f32[4,2,2048]{2,1,0:T(2,128)S(1)}, f32[4,2,2048]{2,1,0:T(2,128)S(1)}) fusion(f32[127,4,2,2048]{0,3,2,1:T(8,128)S(1)} %pad_maximum_fusion), kind=kLoop, calls=%fused_computation.57 | loop fusion | bytes 393216 | tf_op jit(solution)/shard_map/slice | solution.py:55
  133.2 13.4 %copy.210 = f32[124,4,2,2048]{3,2,1,0:T(2,128)} copy(f32[124,4,2,2048]{0,3,2,1:T(8,128)} %bitcast.361) | data formatting | bytes 16252928 | tf_op jit(solution)/shard_map/slice | solution.py:55
  146.6 7.3 broadcast.408.clone
  153.9 447.0 %while.34 = (s32[]{:T(128)}, f32[2,2048]{1,0:T(2,128)S(1)}, f32[4,2,2048]{2,1,0:T(2,128)S(1)}, f32[31,4,2,2048]{3,2,1,0:T(2,128)}, f32[31,4,4,2,2048]{4,3,2,1,0:...) while((s32[]{:T(128)}, f32[2,2048]{1,0:T(2,128)S(1)}, ...), condition=%wide.region_1.2_spmd.clone, body=%wide.region_0.1_spmd.clone.sunk | while | flops 548874 | bytes 1466900 | solution.py:55
  158.3 4.9 broadcast_divide_fusion.12
  187.2 4.9 broadcast_divide_fusion.12
  201.6 4.9 broadcast_divide_fusion.12
  216.0 4.9 broadcast_divide_fusion.12
  230.4 4.9 broadcast_divide_fusion.12
  244.8 4.9 broadcast_divide_fusion.12
  259.2 4.9 broadcast_divide_fusion.12
  273.6 4.9 broadcast_divide_fusion.12
  288.1 4.9 broadcast_divide_fusion.12
  316.9 4.9 broadcast_divide_fusion.12
  331.3 4.9 broadcast_divide_fusion.12
  345.7 4.9 broadcast_divide_fusion.12
  374.6 4.9 broadcast_divide_fusion.12
  389.0 4.9 broadcast_divide_fusion.12
  403.4 4.9 broadcast_divide_fusion.12
  417.9 4.9 broadcast_divide_fusion.12
  609.7 8.3 pad_maximum_fusion.2
  618.1 7.3 broadcast.408
  625.4 86.7 %while.35 = (s32[]{:T(128)}, f32[4,2,2048]{2,1,0:T(2,128)S(1)}, f32[31,4,4,2,2048]{4,3,2,1,0:T(2,128)}, f32[31,4,4,2,2048]{4,3,2,1,0:T(2,128)}, f32[31,4,2,2048]...) while((s32[]{:T(128)}, f32[4,2,2048]{2,1,0:T(2,128)S(1)}, ...), condition=%wide.region_3.4_spmd.clone, body=%wide.region_2.3_spmd.clone.sunk | while | flops 376839 | bytes 1458395 | solution.py:64
  722.4 6.3 fusion.27
  751.3 5.5 collective-permute-start.5
  756.9 7.9 pad_maximum_fusion.1
  771.9 6.4 fusion.30
  821.2 10.5 %copy.227 = f32[2,2,128,2048]{2,1,0,3:T(2,128)S(1)} copy(f32[2,2,128,2048]{2,3,1,0:T(8,128)S(1)} %maximum_bitcast_fusion.3) | data formatting | bytes 8388608 | tf_op jit(solution)/shard_map/transpose | solution.py:183
  831.7 59.8 %all_to_all.33 = f32[2,2,128,2048]{2,1,0,3:T(2,128)S(1)} all-to-all(f32[2,2,128,2048]{2,1,0,3:T(2,128)S(1)} %copy.227), channel_id=1, replica_groups=mesh['span'=16,'wall'=8] {'span'}, dimensions={3} | all-to-all | bytes 8388608 | tf_op jit(solution)/shard_map/all_to_all | solution.py:184
  893.7 5.3 copy.229
  (497 shorter events, 524.9 us)
Async XLA Ops:
  4.7 70.2 %all-to-all-start = ((f32[2,32,128,128]{3,2,0,1:T(8,128)}), f32[2,32,128,128]{3,2,0,1:T(8,128)}, u32[]{:S(2)}, u32[]{:S(2)}) async-start(f32[2,32,128,128]{3,2,0,1:T(8,128)} %copy.196), calls=%async_computation | async-start | bytes 8388608 | tf_op jit(solution)/shard_map/all_to_all | solution.py:129
  92.6 4.9 copy-start.2
  117.0 2.0 copy-start.1
  119.6 13.7 %copy-start = (f32[127,4,2,2048]{0,3,2,1:T(8,128)}, f32[127,4,2,2048]{0,3,2,1:T(8,128)S(1)}, u32[]{:S(2)}) copy-start(f32[127,4,2,2048]{0,3,2,1:T(8,128)S(1)} %pad_maximum_fusion) | copy-start | bytes 24969220
  715.5 13.3 %collective-permute-start = (f32[4,2,2048]{2,1,0:T(2,128)S(1)}, f32[4,2,2048]{2,1,0:T(2,128)S(1)}, u32[]{:S(2)}, u32[]{:S(2)}) collective-permute-start(f32[4,2,2048]{2,1,0:T(2,128)S(1)} %fusion.86), channel_id=1, source_target_pairs={{1,0},{2,1},{3,2},{4,3},{5,4},{6,5},{7,6},{9,8},{10,9},{11,10},{12... | collective-permute-start | bytes 196616 | tf_op jit(solution)/shard_map/ppermute | solution.py:15
  732.1 5.0 collective-permute-start.1
  735.1 5.8 collective-permute-start.2
  741.0 4.7 collective-permute-start.3
  744.2 5.7 collective-permute-start.4
  750.0 14.7 %collective-permute-start.6 = (f32[5,2,2048]{2,1,0:T(2,128)S(1)}, f32[5,2,2048]{2,1,0:T(2,128)S(1)}, u32[]{:S(2)}, u32[]{:S(2)}) collective-permute-start(f32[5,2,2048]{2,1,0:T(2,128)S(1)} %pad_maximum_fusion.11), channel_id=1, source_target_pairs={{4,0},{5,1},{6,2},{7,3},{12,8},{13,9},{14,10},{15,11},{20,16},{21,... | collective-permute-start | bytes 245768 | tf_op jit(solution)/shard_map/ppermute | solution.py:15
  751.3 13.4 %collective-permute-start.5 = (f32[5,2,2048]{2,1,0:T(2,128)S(1)}, f32[5,2,2048]{2,1,0:T(2,128)S(1)}, u32[]{:S(2)}, u32[]{:S(2)}) collective-permute-start(f32[5,2,2048]{2,1,0:T(2,128)S(1)} %pad_maximum_fusion.11), channel_id=1, source_target_pairs={{0,4},{1,5},{2,6},{3,7},{8,12},{9,13},{10,14},{11,15},{16,20},{17,... | collective-permute-start | bytes 245768 | tf_op jit(solution)/shard_map/ppermute | solution.py:15
  756.8 12.1 %slice-start = ((s8[8126464]{0:T(1024)(128)(4,1)}), s8[4194304]{0:T(1024)(128)(4,1)S(1)}, s32[]{:S(2)}) async-start(s8[8126464]{0:T(1024)(128)(4,1)} %bitcast.367), calls=%async_computation.2 | async-start | bytes 8388608
  756.9 12.1 %slice-start.1 = ((s8[8126464]{0:T(1024)(128)(4,1)}), s8[3932160]{0:T(1024)(128)(4,1)S(1)}, s32[]{:S(2)}) async-start(s8[8126464]{0:T(1024)(128)(4,1)} %bitcast.367), calls=%async_computation.3 | async-start | bytes 7864320
  764.8 7.1 collective-permute-start.7
  796.8 4.9 copy-start.3
where the time goes:
time: 916 us; the launch traced here: 899 us
  other arithmetic  449 us (49%)
  local copies, waits for them, and re-layouts  154 us (17%)
  loops' own time  77 us (8%)
  waiting for transfers between devices  61.4 us (7%)
  matrix products  60.8 us (7%)
  blocking collectives  59.8 us (7%)
  starting transfers between devices  33.2 us (4%)
    div x31, other arithmetic, forward(): ratio_new = -upp_entry / pivot_value  153 us
    div x31, other arithmetic, forward(): value_new = (row_now + low_entry * value_prev) / pivot_value  109 us
    slice x96, local copies, waits for them, and re-layouts, thomas(): lax.scan(forward, start_state, (lower_band, upper_band, weight, rows), un...  88.1 us
    another operation x1, loops' own time, thomas(): lax.scan(forward, start_state, (lower_band, upper_band, weight, rows), un...  76.8 us
    dynamic_update_slice x93, other arithmetic, thomas(): lax.scan(forward, start_state, (lower_band, upper_band, weight, rows), un...  72.8 us
    all_to_all x1, blocking collectives, body(): lax.all_to_all(physical, 'span', split_axis=3, concat_axis=1, tiled=True)  59.8 us
    all_to_all x1, waiting for transfers between devices, body(): lax.all_to_all(stress, 'span', split_axis=1, concat_axis=3, tiled=True)  54 us
    broadcast_in_dim x32, other arithmetic, thomas(): lax.scan(backward, jnp.zeros(rows.shape[1:], jnp.float32), sweeps, revers...  32.1 us
  transfers between devices with their start and end apart: 9, of which 4 were waited for; matrix products, arithmetic and copies ran while one was open for 3% of the time, Pallas kernels for 0%

commit v1 on v0

--- a/solution.py
+++ b/solution.py
@@ -7,6 +7,18 @@
 stretch_rate = 2.0
 span_rate = 2.0 / 3.0
 stream_rate = 0.25
+
+
+def in_blocks(array, dim, size):
+    dims = array.shape
+    parts = array.reshape(*dims[:dim], size, dims[dim] // size, *dims[dim + 1 :])
+    return jnp.moveaxis(parts, dim, 0)
+
+
+def laid_out(pieces, dim):
+    shape = list(pieces.shape[1:])
+    shape[dim] *= pieces.shape[0]
+    return jnp.moveaxis(pieces, 0, dim).reshape(shape)
 
 
 def shifted(array, axis, by):
@@ -126,7 +138,14 @@
     weight = lax.dynamic_slice_in_dim(weight_all, row_start, rows_dev)
     mode_ids = span_at * mode_dev + jnp.arange(mode_dev, dtype=jnp.int32)
     wave_sq, span_sq = wave_squares(length, length, mode_ids)
-    received = lax.all_to_all(stress, "span", split_axis=1, concat_axis=3, tiled=True)
+    size, mine = (lax.axis_size("span"), lax.axis_index("span"))
+    blocks = in_blocks(stress, 1, size)
+    outs = [blocks[mine]]
+    for step in range(1, size):
+        sent = blocks[(mine + step) % size]
+        outs.append(lax.ppermute(sent, "span", [(i_2, (i_2 + step) % size) for i_2 in range(size)]))
+    blocks = jnp.stack(outs)[(mine - jnp.arange(size)) % size]
+    received = laid_out(blocks, 3)
     real_part, imag_part = factored_dft(received[0], received[1], -1.0)
     stacked = jnp.stack([real_part, imag_part], axis=0)
     spectral = jnp.transpose(stacked, (2, 0, 1, 3))

time: 916 us -> 967 us (1.056)
  starting transfers between devices: 33.2 us -> 69.6 us
  local copies, waits for them, and re-layouts: 154 us -> 176 us
  waiting for transfers between devices: 61.4 us -> 51.1 us
    all_to_all x1 -> x0, waiting for transfers between devices: 54 us -> none  [body(): lax.all_to_all(stress, 'span', split_axis=1, concat_axis=3, tiled=True)]
    ppermute x0 -> x15, waiting for transfers between devices: none -> 43.7 us  [body(): lax.ppermute(sent, 'span', [(i_2, (i_2 + step) % size) for i_2 in range(s...]
    ppermute x0 -> x15, starting transfers between devices: none -> 28.4 us  [body(): lax.ppermute(sent, 'span', [(i_2, (i_2 + step) % size) for i_2 in range(s...]
    ppermute x8, starting transfers between devices: 24.5 us -> 41.3 us  [shifted(): return lax.ppermute(array, axis, pairs)]
    unnamed x14 -> x28, local copies, waits for them, and re-layouts: 9.09 us -> 20 us
  transfers between devices with their start and end apart: 9 -> 23, of which waited for: 4 -> 12; matrix products, arithmetic and copies ran while one was open for 3% -> 4% of each run, Pallas kernels for 0% -> 0%
where the time goes in v1:
time: 967 us; the launch traced here: 951 us
  other arithmetic  454 us (47%)
  local copies, waits for them, and re-layouts  176 us (18%)
  loops' own time  77.4 us (8%)
  starting transfers between devices  69.6 us (7%)
  matrix products  60.8 us (6%)
  blocking collectives  57.4 us (6%)
  waiting for transfers between devices  51.1 us (5%)
    div x31, other arithmetic, forward(): ratio_new = -upp_entry / pivot_value  158 us
    div x31, other arithmetic, forward(): value_new = (row_now + low_entry * value_prev) / pivot_value  110 us
    slice x96, local copies, waits for them, and re-layouts, thomas(): lax.scan(forward, start_state, (lower_band, upper_band, weight, rows), un...  89 us
    another operation x1, loops' own time, thomas(): lax.scan(forward, start_state, (lower_band, upper_band, weight, rows), un...  77.2 us
    dynamic_update_slice x93, other arithmetic, thomas(): lax.scan(forward, start_state, (lower_band, upper_band, weight, rows), un...  72.9 us
    all_to_all x1, blocking collectives, body(): lax.all_to_all(physical, 'span', split_axis=3, concat_axis=1, tiled=True)  57.4 us
    ppermute x15, waiting for transfers between devices, body(): lax.ppermute(sent, 'span', [(i_2, (i_2 + step) % size) for i_2 in range(s...  43.7 us
    ppermute x8, starting transfers between devices, shifted(): return lax.ppermute(array, axis, pairs)  41.3 us
  transfers between devices with their start and end apart: 23, of which 12 were waited for; matrix products, arithmetic and copies ran while one was open for 4% of the time, Pallas kernels for 0%

profile of v1, /device:TPU:1, one launch (start us, length us, event | category | flops | bytes accessed | tf_op | source)
XLA Modules:
  0.0 950.8 jit_solution(3416178161019128784)
XLA Ops:
  3.2 7.0 collective-permute-start.14
  22.9 16.3 %collective-permute-done = f32[2,2,128,128]{3,2,1,0:T(8,128)} collective-permute-done((f32[2,2,128,128]{3,2,1,0:T(8,128)}, f32[2,2,128,128]{3,2,1,0:T(8,128)}, u32[]{:S(2)}, u32[]{:S(2)}) %collective-permute-start) | collective-permute-done | bytes 262176 | tf_op jit(solution)/shard_map/ppermute | solution.py:146
  59.7 6.4 collective-permute-done.5
  79.6 5.3 collective-permute-start.10
  89.0 5.6 collective-permute-done.11
  150.1 13.5 %slice_reduce_fusion.2 = (f32[4,2,2048]{2,1,0:T(2,128)S(1)}, f32[4,2,2048]{2,1,0:T(2,128)S(1)}, f32[4,2,2048]{2,1,0:T(2,128)S(1)}) fusion(f32[127,4,2,2048]{0,3,2,1:T(8,128)S(1)} %pad_maximum_fusion), kind=kLoop, calls=%fused_computation.58 | loop fusion | bytes 393216 | tf_op jit(solution)/shard_map/slice | solution.py:67
  163.6 13.3 %copy.304 = f32[124,4,2,2048]{3,2,1,0:T(2,128)} copy(f32[124,4,2,2048]{0,3,2,1:T(8,128)} %bitcast.456) | data formatting | bytes 16252928 | tf_op jit(solution)/shard_map/slice | solution.py:67
  176.9 7.3 broadcast.486.clone
  184.2 453.3 %while.34 = (s32[]{:T(128)}, f32[2,2048]{1,0:T(2,128)S(1)}, f32[4,2,2048]{2,1,0:T(2,128)S(1)}, f32[31,4,2,2048]{3,2,1,0:T(2,128)}, f32[31,4,4,2,2048]{4,3,2,1,0:...) while((s32[]{:T(128)}, f32[2,2048]{1,0:T(2,128)S(1)}, ...), condition=%wide.region_1.2_spmd.clone, body=%wide.region_0.1_spmd.clone.sunk | while | flops 548874 | bytes 1466900 | solution.py:67
  188.7 5.1 broadcast_divide_fusion.12
  203.3 5.1 broadcast_divide_fusion.12
  217.9 5.1 broadcast_divide_fusion.12
  232.5 5.1 broadcast_divide_fusion.12
  276.4 5.1 broadcast_divide_fusion.12
  408.0 5.1 broadcast_divide_fusion.12
  422.6 5.1 broadcast_divide_fusion.12
  451.9 5.1 broadcast_divide_fusion.12
  466.5 5.1 broadcast_divide_fusion.12
  495.8 5.1 broadcast_divide_fusion.12
  583.5 5.1 broadcast_divide_fusion.12
  612.7 5.1 broadcast_divide_fusion.12
  646.5 8.6 pad_maximum_fusion.2
  655.1 7.3 broadcast.486
  662.4 86.7 %while.35 = (s32[]{:T(128)}, f32[4,2,2048]{2,1,0:T(2,128)S(1)}, f32[31,4,4,2,2048]{4,3,2,1,0:T(2,128)}, f32[31,4,4,2,2048]{4,3,2,1,0:T(2,128)}, f32[31,4,2,2048]...) while((s32[]{:T(128)}, f32[4,2,2048]{2,1,0:T(2,128)S(1)}, ...), condition=%wide.region_3.4_spmd.clone, body=%wide.region_2.3_spmd.clone.sunk | while | flops 376839 | bytes 1458395 | solution.py:76
  752.5 21.0 %collective-permute-start.15 = (f32[4,2,2048]{2,1,0:T(2,128)S(1)}, f32[4,2,2048]{2,1,0:T(2,128)S(1)}, u32[]{:S(2)}, u32[]{:S(2)}) collective-permute-start(f32[4,2,2048]{2,1,0:T(2,128)S(1)} %fusion.86), channel_id=1, source_target_pairs={{1,0},{2,1},{3,2},{4,3},{5,4},{6,5},{7,6},{9,8},{10,9},{11,10},{12... | collective-permute-start | bytes 196616 | tf_op jit(solution)/shard_map/ppermute | solution.py:27
  776.2 6.4 fusion.27
  805.2 5.5 collective-permute-start.20
  810.7 7.9 pad_maximum_fusion.1
  825.7 6.4 fusion.30
  874.8 10.5 %copy.321 = f32[2,2,128,2048]{2,1,0,3:T(2,128)S(1)} copy(f32[2,2,128,2048]{2,3,1,0:T(8,128)S(1)} %maximum_bitcast_fusion.3) | data formatting | bytes 8388608 | tf_op jit(solution)/shard_map/transpose | solution.py:202
  885.3 57.4 %all_to_all.18 = f32[2,2,128,2048]{2,1,0,3:T(2,128)S(1)} all-to-all(f32[2,2,128,2048]{2,1,0,3:T(2,128)S(1)} %copy.321), channel_id=1, replica_groups=mesh['span'=16,'wall'=8] {'span'}, dimensions={3} | all-to-all | bytes 8388608 | tf_op jit(solution)/shard_map/all_to_all | solution.py:203
  945.0 5.3 copy.323
  (543 shorter events, 597.1 us)
Async XLA Ops:
  3.2 95.4 %collective-permute-start.14 = (f32[2,2,128,128]{3,2,1,0:T(8,128)S(1)}, f32[2,2,128,128]{3,2,1,0:T(8,128)}, u32[]{:S(2)}, u32[]{:S(2)}) collective-permute-start(f32[2,2,128,128]{3,2,1,0:T(8,128)S(1)} %get-tuple-element.416), channel_id=1, source_target_pairs={{0,120},{8,0},{16,8},{24,16},{32,24},{40,32},{48,40},{56,48},{64,5... | collective-permute-start | bytes 786440 | tf_op jit(solution)/shard_map/ppermute | solution.py:146
  10.2 86.7 %collective-permute-start.13 = (f32[2,2,128,128]{3,2,1,0:T(8,128)S(1)}, f32[2,2,128,128]{3,2,1,0:T(8,128)}, u32[]{:S(2)}, u32[]{:S(2)}) collective-permute-start(f32[2,2,128,128]{3,2,1,0:T(8,128)S(1)} %get-tuple-element.417), channel_id=1, source_target_pairs={{0,112},{8,120},{16,0},{24,8},{32,16},{40,24},{48,32},{56,40},{64,... | collective-permute-start | bytes 786440 | tf_op jit(solution)/shard_map/ppermute | solution.py:146
  10.2 85.0 %collective-permute-start.12 = (f32[2,2,128,128]{3,2,1,0:T(8,128)S(1)}, f32[2,2,128,128]{3,2,1,0:T(8,128)}, u32[]{:S(2)}, u32[]{:S(2)}) collective-permute-start(f32[2,2,128,128]{3,2,1,0:T(8,128)S(1)} %get-tuple-element.418), channel_id=1, source_target_pairs={{0,104},{8,112},{16,120},{24,0},{32,8},{40,16},{48,24},{56,32},{64... | collective-permute-start | bytes 786440 | tf_op jit(solution)/shard_map/ppermute | solution.py:146
  11.1 31.9 %collective-permute-start.1 = (f32[2,2,128,128]{3,2,1,0:T(8,128)}, f32[2,2,128,128]{3,2,1,0:T(8,128)}, u32[]{:S(2)}, u32[]{:S(2)}) collective-permute-start(f32[2,2,128,128]{3,2,1,0:T(8,128)} %get-tuple-element.429), channel_id=1, source_target_pairs={{0,16},{8,24},{16,32},{24,40},{32,48},{40,56},{48,64},{56,72},{64,... | collective-permute-start | bytes 786440 | tf_op jit(solution)/shard_map/ppermute | solution.py:146
  13.2 26.1 %collective-permute-start = (f32[2,2,128,128]{3,2,1,0:T(8,128)}, f32[2,2,128,128]{3,2,1,0:T(8,128)}, u32[]{:S(2)}, u32[]{:S(2)}) collective-permute-start(f32[2,2,128,128]{3,2,1,0:T(8,128)} %get-tuple-element.430), channel_id=1, source_target_pairs={{0,8},{8,16},{16,24},{24,32},{32,40},{40,48},{48,56},{56,64},{64,7... | collective-permute-start | bytes 786440 | tf_op jit(solution)/shard_map/ppermute | solution.py:146
  39.2 8.0 collective-permute-start.2
  43.0 8.3 collective-permute-start.3
  47.2 9.5 %collective-permute-start.4 = (f32[2,2,128,128]{3,2,1,0:T(8,128)S(1)}, f32[2,2,128,128]{3,2,1,0:T(8,128)S(1)}, u32[]{:S(2)}, u32[]{:S(2)}) collective-permute-start(f32[2,2,128,128]{3,2,1,0:T(8,128)S(1)} %get-tuple-element.426), channel_id=1, source_target_pairs={{0,40},{8,48},{16,56},{24,64},{32,72},{40,80},{48,88},{56,96},{64,... | collective-permute-start | bytes 786440 | tf_op jit(solution)/shard_map/ppermute | solution.py:146
  51.2 14.9 %collective-permute-start.5 = (f32[2,2,128,128]{3,2,1,0:T(8,128)S(1)}, f32[2,2,128,128]{3,2,1,0:T(8,128)S(1)}, u32[]{:S(2)}, u32[]{:S(2)}) collective-permute-start(f32[2,2,128,128]{3,2,1,0:T(8,128)S(1)} %get-tuple-element.425), channel_id=1, source_target_pairs={{0,48},{8,56},{16,64},{24,72},{32,80},{40,88},{48,96},{56,104},{64... | collective-permute-start | bytes 786440 | tf_op jit(solution)/shard_map/ppermute | solution.py:146
  56.8 10.9 %collective-permute-start.6 = (f32[2,2,128,128]{3,2,1,0:T(8,128)S(1)}, f32[2,2,128,128]{3,2,1,0:T(8,128)S(1)}, u32[]{:S(2)}, u32[]{:S(2)}) collective-permute-start(f32[2,2,128,128]{3,2,1,0:T(8,128)S(1)} %get-tuple-element.424), channel_id=1, source_target_pairs={{0,56},{8,64},{16,72},{24,80},{32,88},{40,96},{48,104},{56,112},{6... | collective-permute-start | bytes 786440 | tf_op jit(solution)/shard_map/ppermute | solution.py:146
  66.1 8.4 collective-permute-start.7
  67.7 11.9 %collective-permute-start.8 = (f32[2,2,128,128]{3,2,1,0:T(8,128)S(1)}, f32[2,2,128,128]{3,2,1,0:T(8,128)S(1)}, u32[]{:S(2)}, u32[]{:S(2)}) collective-permute-start(f32[2,2,128,128]{3,2,1,0:T(8,128)S(1)} %get-tuple-element.422), channel_id=1, source_target_pairs={{0,72},{8,80},{16,88},{24,96},{32,104},{40,112},{48,120},{56,0},{6... | collective-permute-start | bytes 786440 | tf_op jit(solution)/shard_map/ppermute | solution.py:146
  74.5 11.1 %collective-permute-start.9 = (f32[2,2,128,128]{3,2,1,0:T(8,128)S(1)}, f32[2,2,128,128]{3,2,1,0:T(8,128)S(1)}, u32[]{:S(2)}, u32[]{:S(2)}) collective-permute-start(f32[2,2,128,128]{3,2,1,0:T(8,128)S(1)} %get-tuple-element.421), channel_id=1, source_target_pairs={{0,80},{8,88},{16,96},{24,104},{32,112},{40,120},{48,0},{56,8},{64... | collective-permute-start | bytes 786440 | tf_op jit(solution)/shard_map/ppermute | solution.py:146
  79.6 8.6 collective-permute-start.10
  85.6 8.9 collective-permute-start.11
  123.1 4.9 copy-start.2
  147.5 2.0 copy-start.1
  150.1 13.5 %copy-start = (f32[127,4,2,2048]{0,3,2,1:T(8,128)}, f32[127,4,2,2048]{0,3,2,1:T(8,128)S(1)}, u32[]{:S(2)}) copy-start(f32[127,4,2,2048]{0,3,2,1:T(8,128)S(1)} %pad_maximum_fusion) | copy-start | bytes 24969220
  752.5 30.1 %collective-permute-start.15 = (f32[4,2,2048]{2,1,0:T(2,128)S(1)}, f32[4,2,2048]{2,1,0:T(2,128)S(1)}, u32[]{:S(2)}, u32[]{:S(2)}) collective-permute-start(f32[4,2,2048]{2,1,0:T(2,128)S(1)} %fusion.86), channel_id=1, source_target_pairs={{1,0},{2,1},{3,2},{4,3},{5,4},{6,5},{7,6},{9,8},{10,9},{11,10},{12... | collective-permute-start | bytes 196616 | tf_op jit(solution)/shard_map/ppermute | solution.py:27
  785.9 5.0 collective-permute-start.16
  789.0 5.8 collective-permute-start.17
  794.9 4.7 collective-permute-start.18
  798.1 5.7 collective-permute-start.19
  803.9 14.7 %collective-permute-start.21 = (f32[5,2,2048]{2,1,0:T(2,128)S(1)}, f32[5,2,2048]{2,1,0:T(2,128)S(1)}, u32[]{:S(2)}, u32[]{:S(2)}) collective-permute-start(f32[5,2,2048]{2,1,0:T(2,128)S(1)} %pad_maximum_fusion.11), channel_id=1, source_target_pairs={{4,0},{5,1},{6,2},{7,3},{12,8},{13,9},{14,10},{15,11},{20,16},{21,... | collective-permute-start | bytes 245768 | tf_op jit(solution)/shard_map/ppermute | solution.py:27
  805.2 13.4 %collective-permute-start.20 = (f32[5,2,2048]{2,1,0:T(2,128)S(1)}, f32[5,2,2048]{2,1,0:T(2,128)S(1)}, u32[]{:S(2)}, u32[]{:S(2)}) collective-permute-start(f32[5,2,2048]{2,1,0:T(2,128)S(1)} %pad_maximum_fusion.11), channel_id=1, source_target_pairs={{0,4},{1,5},{2,6},{3,7},{8,12},{9,13},{10,14},{11,15},{16,20},{17,... | collective-permute-start | bytes 245768 | tf_op jit(solution)/shard_map/ppermute | solution.py:27
  810.7 12.1 %slice-start = ((s8[8126464]{0:T(1024)(128)(4,1)}), s8[4194304]{0:T(1024)(128)(4,1)S(1)}, s32[]{:S(2)}) async-start(s8[8126464]{0:T(1024)(128)(4,1)} %bitcast.462), calls=%async_computation.1 | async-start | bytes 8388608
  810.7 12.1 %slice-start.1 = ((s8[8126464]{0:T(1024)(128)(4,1)}), s8[3932160]{0:T(1024)(128)(4,1)S(1)}, s32[]{:S(2)}) async-start(s8[8126464]{0:T(1024)(128)(4,1)} %bitcast.462), calls=%async_computation.2 | async-start | bytes 7864320
  818.7 7.0 collective-permute-start.22
  850.4 4.9 copy-start.3
